TPU v7x, 32 devices: a whole 2x2x4 slice. The times are simulated.
32 devices in a mesh: dp: 8 (over y, x, core), expert: 4 (over z).
Axes of the slice: x: 2, y: 2, z: 4, core: 2. Of those that a mesh axis runs over, the one named last changes fastest.
Arguments:
- out_grad: bfloat16 [512, 4096], P('expert', 'dp'), may hold values from -6 to 6
- logits: float32 [512, 16], P('expert'), may hold values from -12 to 12
- routes: int32 [512, 8], P('expert'), may hold values from 0 to 15, all different within a row; in each aligned block of 128 rows (0 to 127, 128 to 255, ...) at most 96 rows name the same one
- hidden: bfloat16 [16, 384, 1536], P('expert'), may hold values from -6 to 6
- w_down: bfloat16 [16, 1536, 4096], P('expert', None, 'dp'), may hold values from -0.15625 to 0.15625
Outputs:
- grad_down: bfloat16 [16, 1536, 4096], P('expert', None, 'dp')
- grad_hidden: bfloat16 [384, 16, 1536], P('dp', 'expert')
- grad_logits: float32 [512, 16], P('expert')
Inputs may be any that keep to these rules, and one draw needn't show every extreme that they name: `routes`: within the 128 rows of one device no expert is named more than 96 times, a bound that some block reaches; the experts of one row differ.
All inputs are finite; a program needn't handle non-finite values.
Results may differ from a plain program's by a relative error of at most 0.0057.
Values may be sent and summed in bfloat16 or wider, within the bound.
A program may use at most 64 MiB of HBM per device.

v0:
```python
import jax
import jax.numpy as jnp
from jax import lax
from jax.sharding import PartitionSpec as P


def per_device(out_grad, logits, routes, hidden, w_down):
    tok_rows = out_grad.shape[0]
    top_count = routes.shape[1]
    n_experts = logits.shape[1]
    slot_count = hidden.shape[1]
    n_source = lax.axis_size("expert")
    capacity = slot_count // n_source
    feat_cols = out_grad.shape[1]
    probs = jax.nn.softmax(logits, axis=-1)
    sel = jnp.take_along_axis(probs, routes, axis=1)
    wsum = jnp.sum(sel, axis=1)
    comb = sel / wsum[:, None]
    comb_b = comb.astype(jnp.bfloat16)
    flat_routes = routes.reshape(-1)
    onehot = (flat_routes[:, None] == jnp.arange(n_experts, dtype=jnp.int32)[None, :]).astype(
        jnp.int32
    )
    before = jnp.cumsum(onehot, axis=0) - onehot
    rank = jnp.sum(before * onehot, axis=1)
    target = flat_routes * capacity + rank
    repeated = jnp.repeat(out_grad, top_count, axis=0)
    send_rows = jnp.zeros((n_experts * capacity, feat_cols), jnp.bfloat16).at[target].set(repeated)
    send_rows = send_rows.reshape(n_experts, capacity, feat_cols)
    send_wts = jnp.zeros((n_experts * capacity,), jnp.bfloat16).at[target].set(comb_b.reshape(-1))
    send_wts = send_wts.reshape(n_experts, capacity)
    recv_rows, recv_wts = (
        lax.all_to_all(send_rows, "expert", split_axis=0, concat_axis=1, tiled=True),
        lax.all_to_all(send_wts, "expert", split_axis=0, concat_axis=1, tiled=True),
    )
    wts_f = recv_wts.astype(jnp.float32)
    scaled = (wts_f[:, :, None] * recv_rows.astype(jnp.float32)).astype(jnp.bfloat16)
    grad_down = jnp.einsum(
        "esf,esd->efd", hidden, scaled, preferred_element_type=jnp.float32
    ).astype(jnp.bfloat16)
    own_count = slot_count // lax.axis_size("dp")
    own_sums = lax.psum_scatter(
        jnp.einsum("esd,efd->sef", recv_rows, w_down, preferred_element_type=jnp.float32),
        "dp",
        scatter_dimension=0,
        tiled=True,
    )
    own_start = lax.axis_index("dp") * own_count
    own_wts = lax.dynamic_slice_in_dim(wts_f, own_start, own_count, 1)
    grad_hidden = (jnp.transpose(own_wts)[:, :, None] * own_sums).astype(jnp.bfloat16)
    outputs = jnp.einsum("esf,efd->esd", hidden, w_down, preferred_element_type=jnp.float32)
    local_part = jnp.sum(outputs * recv_rows.astype(jnp.float32), axis=2)
    dslot = lax.psum(local_part, "dp")
    returned = lax.all_to_all(dslot, "expert", split_axis=1, concat_axis=0, tiled=True)
    dcomb = returned.reshape(-1)[target].reshape(tok_rows, top_count)
    dsel = (dcomb - jnp.sum(comb * dcomb, axis=1, keepdims=True)) / wsum[:, None]
    spread = jnp.sum(
        onehot.astype(jnp.float32).reshape(tok_rows, top_count, n_experts) * dsel[:, :, None],
        axis=1,
    )
    grad_logits = probs * (spread - jnp.sum(sel * dsel, axis=1, keepdims=True))
    return (grad_down, grad_hidden, grad_logits)


def solution(mesh):
    return jax.shard_map(
        per_device,
        mesh=mesh,
        in_specs=(
            P("expert", "dp"),
            P("expert", None),
            P("expert", None),
            P("expert", None, None),
            P("expert", None, "dp"),
        ),
        out_specs=(P("expert", None, "dp"), P("dp", "expert", None), P("expert", None)),
        check_vma=False,
    )
```

profile of v0, /device:TPU:0, one launch (start us, length us, event | category | flops | bytes accessed | tf_op | source)
XLA Modules:
  0.0 158.5 jit_solution(9620357304133136882)
XLA Ops:
  7.2 0.8 copy.82
  8.0 0.1 eq.36
  8.2 0.7 broadcast_multiply_fusion
  8.9 4.5 %reduce-window.6 = s32[16,8,128]{2,1,0:T(8,128)S(1)} reduce-window(s32[16,8,128]{2,1,0:T(8,128)S(1)} %fusion.11, s32[]{:T(128)} %constant.15.clone.1), window={size=1x1x128 pad=0_0x0_0x127_0}, to_apply=%region_0.0 | reduce-window | flops 2080768 | bytes 131076 | tf_op jit(solution)/shard_map/reduce-window
  13.5 0.1 copy.84
  13.9 0.1 copy.81
  14.0 0.1 mul.60
  14.1 5.6 %scatter_custom_fusion.1 = bf16[1536,512]{1,0:T(8,128)(2,1)S(1)} fusion(s32[1024]{0:T(1024)S(1)} %bitcast.55, bf16[]{:T(256)} %constant.13.clone.1, bf16[128,512]{1,0:T(8,128)(2,1)S(1)} %copy-done), kind=kCustom, calls=%fused_computation.12 | custom fusion | bytes 1703938 | tf_op jit(solution)/shard_map/scatter | solution.py:28
  19.7 43.3 %all_to_all.47 = bf16[16,96,512]{2,1,0:T(8,128)(2,1)S(1)} all-to-all(bf16[16,96,512]{2,1,0:T(8,128)(2,1)S(1)} %bitcast.50), channel_id=1, replica_groups=mesh['dp'=8,'expert'=4] {'expert'}, dimensions={0} | all-to-all | bytes 3145728 | tf_op jit(solution)/shard_map/all_to_all | solution.py:33
  63.0 0.1 copy.90
  63.2 5.1 %convolution_bitcast_fusion = f32[384,4,1536]{2,0,1:T(8,128)} fusion(bf16[4,384,512]{2,1,0:T(8,128)(2,1)S(1)} %bitcast.46, bf16[4,1536,512]{2,1,0:T(8,128)(2,1)S(1)} %copy-done.1), kind=kOutput, calls=%fused_computation.5 | convolution fusion | flops 2415919104 | bytes 17301504 | tf_op jit(solution)/shard_map/esd,efd->sef/dot_general | solution.py:43
  68.3 0.7 copy-done.3
  69.0 0.1 copy.86
  69.1 0.1 reshape.161
  69.2 7.0 %gather_fusion.1 = f32[1024]{0:T(1024)S(1)} fusion(f32[128,16]{0,1:T(8,128)S(1)} %fusion.12, s32[1024]{0:T(1024)S(1)} %reshape.161), kind=kCustom, calls=%fused_computation.1 | custom fusion | bytes 16384 | tf_op jit(solution)/shard_map/jit(take_along_axis)/gather | solution.py:16
  76.4 9.1 %fusion.1 = f32[4,384]{1,0:T(4,128)S(1)} fusion(bf16[4,384,512]{2,1,0:T(8,128)(2,1)S(1)} %bitcast.47, bf16[4,384,1536]{2,1,0:T(8,128)(2,1)} %param.8, bf16[4,1536,512]{2,1,0:T(8,128)(2,1)} %param.9), kind=kOutput, calls=%fused_computation.9 | convolution fusion | flops 2418276864 | bytes 12589056 | tf_op jit(solution)/shard_map/esf,efd->esd/dot_general | solution.py:51
  85.6 13.3 %psum.7 = f32[4,4,96]{2,1,0:T(4,128)S(1)} all-reduce(f32[4,4,96]{2,1,0:T(4,128)S(1)} %all_to_all.41), channel_id=1, replica_groups=mesh['dp'=8,'expert'=4] {'dp'}, use_global_device_ids=true, to_apply=%region_10.11 | all-reduce | flops 1536 | bytes 12288 | tf_op jit(solution)/shard_map/psum | solution.py:53
  98.9 0.6 copy.92
  99.5 3.2 %all-to-all-start.2 = ((f32[4,4,96]{2,0,1:T(4,128)}), f32[4,4,96]{2,0,1:T(4,128)S(1)}, u32[]{:S(2)}, u32[]{:S(2)}) async-start(f32[4,4,96]{2,0,1:T(4,128)} %copy.92), calls=%async_computation.3 | async-start | bytes 16384 | tf_op jit(solution)/shard_map/all_to_all | solution.py:54
  102.8 5.5 %all-to-all-done.2 = f32[4,4,96]{2,0,1:T(4,128)S(1)} async-done(((f32[4,4,96]{2,0,1:T(4,128)}), f32[4,4,96]{2,0,1:T(4,128)S(1)}, u32[]{:S(2)}, u32[]{:S(2)}) %all-to-all-start.2) | async-done | bytes 6176 | tf_op jit(solution)/shard_map/all_to_all | solution.py:54
  108.4 6.1 %gather_fusion = f32[1024]{0:T(1024)S(1)} fusion(f32[1536]{0:T(1024)S(1)} %reshape.150, s32[1024]{0:T(1024)S(1)} %broadcast_clamp_fusion), kind=kCustom, calls=%fused_computation | custom fusion | bytes 12288 | tf_op jit(solution)/shard_map/gather | solution.py:55
  114.8 0.1 copy.88
  114.9 0.1 reshape.171
  115.0 7.6 %scatter_custom_fusion = bf16[1536]{0:T(1024)(128)(2,1)S(1)} fusion(s32[1024]{0:T(1024)S(1)} %bitcast.57, bf16[1024]{0:T(1024)(128)(2,1)S(1)} %reshape.171, bf16[]{:T(256)} %constant.13.clone.1), kind=kCustom, calls=%fused_computation.42 | custom fusion | bytes 3074 | tf_op jit(solution)/shard_map/scatter | solution.py:30
  122.6 0.7 all_to_all.35
  123.3 3.4 %all-to-all-start = ((bf16[4,4,96]{2,1,0:T(4,128)(2,1)}), bf16[4,4,96]{2,1,0:T(4,128)(2,1)S(1)}, u32[]{:S(2)}, u32[]{:S(2)}) async-start(bf16[4,4,96]{2,1,0:T(4,128)(2,1)} %all_to_all.35), calls=%async_computation | async-start | bytes 8192 | tf_op jit(solution)/shard_map/all_to_all | solution.py:34
  126.7 0.6 subtract_multiply_fusion
  127.3 4.9 %all-to-all-done = bf16[4,4,96]{2,1,0:T(4,128)(2,1)S(1)} async-done(((bf16[4,4,96]{2,1,0:T(4,128)(2,1)}), bf16[4,4,96]{2,1,0:T(4,128)(2,1)S(1)}, u32[]{:S(2)}, u32[]{:S(2)}) %all-to-all-start) | async-done | bytes 3104 | tf_op jit(solution)/shard_map/all_to_all | solution.py:34
  132.4 7.8 %convert_bitcast_fusion = bf16[4,1536,512]{1,2,0:T(8,128)(2,1)} fusion(bf16[4,384,1536]{2,1,0:T(8,128)(2,1)} %param.8, bf16[4,384,512]{2,1,0:T(8,128)(2,1)S(1)} %bitcast.48, f32[4,384]{1,0:T(4,128)S(1)} %reshape.152), kind=kOutput, calls=%fused_computation.4 | convolution fusion | flops 2421424128 | bytes 12589056 | tf_op jit(solution)/shard_map/esf,esd->efd/dot_general | solution.py:38
  140.2 8.7 %copy.95 = bf16[4,1536,512]{2,1,0:T(8,128)(2,1)} copy(bf16[4,1536,512]{1,2,0:T(8,128)(2,1)} %convert_bitcast_fusion) | data formatting | bytes 12582912
  149.0 1.4 multiply_convert_fusion
  150.4 1.3 copy.96
  (38 shorter events, 1.2 us)
Async XLA Ops:
  7.2 7.0 %copy-start = (bf16[128,512]{1,0:T(8,128)(2,1)S(1)}, bf16[128,512]{1,0:T(8,128)(2,1)}, u32[]{:S(2)}) copy-start(bf16[128,512]{1,0:T(8,128)(2,1)} %param.5) | copy-start | bytes 393220
  7.2 141.8 %reduce-scatter.2.cloned.1.call-start = ((), (), s32[]{:S(2)}) async-start(), calls=%async_computation.4 | async-start | bytes 10616832 | tf_op jit(solution)/shard_map/reduce_scatter | solution.py:42
  19.7 43.5 %copy-start.1 = (bf16[4,1536,512]{2,1,0:T(8,128)(2,1)S(1)}, bf16[4,1536,512]{2,1,0:T(8,128)(2,1)}, u32[]{:S(2)}) copy-start(bf16[4,1536,512]{2,1,0:T(8,128)(2,1)} %param.9) | copy-start | bytes 18874372
  68.3 0.7 copy-start.3
  68.3 0.9 copy-start.2
  99.5 8.8 %all-to-all-start.2 = ((f32[4,4,96]{2,0,1:T(4,128)}), f32[4,4,96]{2,0,1:T(4,128)S(1)}, u32[]{:S(2)}, u32[]{:S(2)}) async-start(f32[4,4,96]{2,0,1:T(4,128)} %copy.92), calls=%async_computation.3 | async-start | bytes 16384 | tf_op jit(solution)/shard_map/all_to_all | solution.py:54
  123.3 9.0 %all-to-all-start = ((bf16[4,4,96]{2,1,0:T(4,128)(2,1)}), bf16[4,4,96]{2,1,0:T(4,128)(2,1)S(1)}, u32[]{:S(2)}, u32[]{:S(2)}) async-start(bf16[4,4,96]{2,1,0:T(4,128)(2,1)} %all_to_all.35), calls=%async_computation | async-start | bytes 8192 | tf_op jit(solution)/shard_map/all_to_all | solution.py:34
Sparse Core Ops, SparseCore 0:
  68.4 75.6 reduce-scatter.1
where the time goes:
time: 159 us; the launch traced here: 158 us
  blocking collectives  56.6 us (36%)
  local copies, waits for them, and re-layouts  40.8 us (26%)
  matrix products  22 us (14%)
  between operations  14.2 us (9%)
  waiting for transfers between devices  10.5 us (7%)
  other arithmetic  7.55 us (5%)
  starting transfers between devices  6.71 us (4%)
    all_to_all x1, blocking collectives, per_device(): lax.all_to_all(send_rows, 'expert', split_axis=0, concat_axis=1, tiled=True)  43.3 us
    psum x1, blocking collectives, per_device(): dslot = lax.psum(local_part, 'dp')  13.3 us
    unnamed x11, local copies, waits for them, and re-layouts  11.4 us
    dot_general x1, matrix products, per_device(): jnp.einsum('esf,efd->esd', hidden, w_down, preferred_element_type=jnp.flo...  9.09 us
    dot_general x1, matrix products, per_device(): jnp.einsum('esf,esd->efd', hidden, scaled, preferred_element_type=jnp.flo...  7.84 us
    scatter x1, local copies, waits for them, and re-layouts, per_device(): jnp.zeros((n_experts * capacity,), jnp.bfloat16).at[target]  7.59 us
    gather x5, local copies, waits for them, and re-layouts, per_device(): sel = jnp.take_along_axis(probs, routes, axis=1)  7.35 us
    gather x1, local copies, waits for them, and re-layouts, per_device(): dcomb = returned.reshape(-1)[target].reshape(tok_rows, top_count)  6.15 us
  transfers between devices with their start and end apart: 3, of which 2 were waited for; matrix products, arithmetic and copies ran while one was open for 31% of the time, Pallas kernels for 0%

commit v1 on v0

v1 whole, which is shorter than its diff:
```python
import functools

import jax
import jax.numpy as jnp
from jax import lax
from jax.experimental import pallas as pl
from jax.experimental.pallas import tpu as pltpu
from jax.sharding import PartitionSpec as P

MESH = pl.DeviceIdType.MESH
F32, BF16 = jnp.float32, jnp.bfloat16
GROUP = 8


def bit_of(value, b):
    return lax.rem(value // (1 << b), 2) if not isinstance(value, int) else (value >> b) & 1


def flipped(value, b):
    return value + (1 << b) * (1 - 2 * bit_of(value, b))


def stream_bits(levels, expert):
    rest = list(range(1, levels))
    return [0] + (rest if expert % 2 == 0 else rest[::-1])


def relative(position, bits):
    levels = len(bits)
    return sum(((position >> (levels - 1 - k)) & 1) << b for k, b in enumerate(bits))


def kernel(
    nz, nd, own, pad, cap, experts, ft,
    og_ref, lt_ref, rt_ref, hid_hbm, w_hbm,
    gh_ref, gl_ref, scaled_ref,
    w, hid, og, meta, gmeta, onehot, disp, wcol, acc, snd, rcv, dsl, dc, dcr, ret,
    load_sem, og_s, og_r, mt_s, mt_r, rs_s, rs_r, ar_s, ar_r, z_s, z_r,
):
    me_d, me_z = lax.axis_index("dp"), lax.axis_index("expert")
    levels = nd.bit_length() - 1
    rows = nd * pad
    half = rows // 2
    tok = og_ref.shape[0]
    hidden_units = w.shape[1]

    loads = []
    for e in range(experts):
        pair = (
            pltpu.make_async_copy(w_hbm.at[e], w.at[e], load_sem.at[2 * e]),
            pltpu.make_async_copy(hid_hbm.at[e], hid.at[e], load_sem.at[2 * e + 1]),
        )
        for copy in pair:
            copy.start()
        loads.append(pair)

    barrier = pltpu.get_barrier_semaphore()
    for k in range(1, nz):
        pl.semaphore_signal(barrier, inc=1, device_id=(me_d, lax.rem(me_z + k, nz)), device_id_type=MESH)
    for b in range(levels):
        pl.semaphore_signal(barrier, inc=1, device_id=(flipped(me_d, b), me_z), device_id_type=MESH)

    lt = lt_ref[...]
    row = lax.broadcasted_iota(jnp.int32, lt.shape, 0)
    local = lax.rem(row, GROUP)
    eid = jnp.where(local < experts, (row // GROUP) * experts + local, -1)
    top = rt_ref.shape[0]
    chosen = jnp.zeros(lt.shape, F32)
    for k in range(top):
        chosen = jnp.where(rt_ref[k : k + 1, :] == eid, 1.0, chosen)
    raised = jnp.exp(lt - jnp.max(lt, axis=0, keepdims=True))
    probs = raised / jnp.sum(raised, axis=0, keepdims=True)
    sel = probs * chosen
    wsum = jnp.sum(sel, axis=0, keepdims=True)
    comb = sel / wsum
    t2 = lax.broadcasted_iota(jnp.int32, (tok, tok), 0)
    t1 = lax.broadcasted_iota(jnp.int32, (tok, tok), 1)
    earlier = jnp.where(t2 < t1, 1.0, 0.0).astype(BF16)
    rank = jnp.dot(chosen.astype(BF16), earlier, preferred_element_type=F32)
    place = jnp.where(chosen > 0.5, rank, -1.0)
    for z in range(nz):
        part = slice(z * GROUP, (z + 1) * GROUP)
        meta[z] = jnp.concatenate([place[part], comb[part]], axis=0).astype(BF16)

    pl.semaphore_wait(barrier, nz - 1 + levels)
    copies = []
    for k in range(1, nz):
        to = lax.rem(me_z + k, nz)
        copies.append(pltpu.make_async_remote_copy(
            src_ref=og_ref, dst_ref=og.at[me_z], send_sem=og_s.at[k - 1], recv_sem=og_r.at[k - 1],
            device_id=(me_d, to), device_id_type=MESH))
        copies.append(pltpu.make_async_remote_copy(
            src_ref=meta.at[to], dst_ref=gmeta.at[me_z], send_sem=mt_s.at[k - 1], recv_sem=mt_r.at[k - 1],
            device_id=(me_d, to), device_id_type=MESH))
    for copy in copies:
        copy.start()
    og[me_z] = og_ref[...]
    gmeta[me_z] = meta[me_z]

    at = lax.broadcasted_iota(jnp.int32, (rows, tok), 0)
    position, inside = at // pad, lax.rem(at, pad)
    slot_at = []
    for stream in range(2):
        bits = stream_bits(levels, stream)
        owner = jnp.zeros_like(at)
        for k, b in enumerate(bits):
            differs = lax.rem(position // (1 << (levels - 1 - k)), 2)
            owner = owner + (1 << b) * lax.rem(differs + bit_of(me_d, b), 2)
        slot_at.append(jnp.where(inside < own, owner * own + inside, -7).astype(F32))

    def owner_of(p, bits):
        r = relative(p, bits)
        return sum((1 << b) * lax.rem(bit_of(r, b) + bit_of(me_d, b), 2) for b in range(levels))

    for copy in copies:
        copy.wait()

    def rs_copy(e, level):
        bits = stream_bits(levels, e)
        size = rows >> (level + 1)
        start = rows - (rows >> level)
        return pltpu.make_async_remote_copy(
            src_ref=snd.at[e, pl.ds(start, size)], dst_ref=rcv.at[e, pl.ds(start, size)],
            send_sem=rs_s.at[e * levels + level], recv_sem=rs_r.at[e * levels + level],
            device_id=(flipped(me_d, bits[level]), me_z), device_id_type=MESH)

    def compute(e):
        bits = stream_bits(levels, e)
        slots = slot_at[e % 2]
        wcol[e] = jnp.zeros((rows, tok), F32)

        def dispatch(s):
            told = gmeta[s].astype(F32)
            place_row, comb_row = told[e : e + 1], told[GROUP + e : GROUP + e + 1]
            offset = s * cap if isinstance(s, int) else (s * cap).astype(F32)
            absolute = jnp.where(place_row >= 0.0, place_row + offset, -1.0)
            hit = slots == absolute
            lanes = pl.ds(s * tok if isinstance(s, int) else pl.multiple_of(s * tok, tok), tok)
            onehot[e, :, lanes] = jnp.where(hit, 1.0, 0.0).astype(BF16)
            wcol[e] += jnp.where(hit, comb_row, 0.0)

        if nz <= 8:
            for s in range(nz):
                dispatch(s)
        else:
            @pl.loop(0, nz)
            def _(s):
                dispatch(s)

        weight = jnp.sum(wcol[e], axis=1, keepdims=True)
        wcol[e] = jnp.broadcast_to(weight, (rows, tok))
        cols = og.shape[2]
        d = jnp.dot(onehot[e], og[...].reshape(nz * tok, cols), preferred_element_type=F32)
        disp[...] = d.astype(BF16)
        scaled = (weight * d).astype(BF16)
        for p in range(nd):
            scaled_ref[e, owner_of(p, bits)] = scaled[p * pad : (p + 1) * pad]
        for copy in loads[e]:
            copy.wait()
        dsl[...] = jnp.zeros(dsl.shape, F32)

        @pl.loop(0, hidden_units // ft)
        def _(i):
            part = pl.ds(pl.multiple_of(i * ft, ft), ft)
            u = lax.dot_general(disp[...], w[e, part, :], (((1,), (1,)), ((), ())), preferred_element_type=F32)
            acc[e, :, part] = u[:half]
            snd[e, 0:half, part] = u[half:].astype(BF16)
            for p in range(nd):
                prod = u[p * pad : (p + 1) * pad] * hid[e, owner_of(p, bits), :, part].astype(F32)
                total = prod[:, 0:128]
                for c in range(128, ft, 128):
                    total = total + prod[:, c : c + 128]
                dsl[p * pad : (p + 1) * pad, :] += total

        rs_copy(e, 0).start()
        line = jnp.sum(jnp.transpose(dsl[...]), axis=0, keepdims=True)
        high = line.astype(BF16).astype(F32)
        mid = (line - high).astype(BF16).astype(F32)
        low = line - high - mid
        which = lax.broadcasted_iota(jnp.int32, (16, rows), 0)
        three = jnp.where(which == 0, high, jnp.where(which == 1, mid, jnp.where(which == 2, low, 0.0))).astype(BF16)
        back = jnp.dot(three, onehot[e], preferred_element_type=F32)
        back = jnp.sum(back, axis=0, keepdims=True)
        for s in range(nz):
            dc[0, s, e : e + 1, :] = back[:, s * tok : (s + 1) * tok]

    def advance(e, level):
        copy = rs_copy(e, level)
        copy.wait()
        size = rows >> (level + 1)
        start = rows - (rows >> level)
        if level < levels - 1:
            keep = size // 2
            snd[e, start + size : start + size + keep] = (
                acc[e, keep:size] + rcv[e, start + keep : start + size].astype(F32)).astype(BF16)
            rs_copy(e, level + 1).start()
            acc[e, 0:keep] += rcv[e, start : start + keep].astype(F32)
        else:
            total = acc[e, 0:size] + rcv[e, start : start + size].astype(F32)
            gh_ref[e] = (wcol[e, 0:size, 0:1] * total).astype(BF16)

    def ar_copy(level):
        return pltpu.make_async_remote_copy(
            src_ref=dc.at[level], dst_ref=dcr.at[level], send_sem=ar_s.at[level], recv_sem=ar_r.at[level],
            device_id=(flipped(me_d, level), me_z), device_id_type=MESH)

    dc[0] = jnp.zeros(dc.shape[1:], F32)
    compute(0)
    for e in range(1, experts):
        compute(e)
        advance(e - 1, 0)

    def ar_step(level):
        ar_copy(level).wait()
        dc[level + 1] = dc[level] + dcr[level]

    ar_copy(0).start()
    advance(experts - 1, 0)
    for level in range(levels):
        ar_step(level)
        if level + 1 < levels:
            ar_copy(level + 1).start()
    returns = []
    for k in range(1, nz):
        to = lax.rem(me_z + k, nz)
        returns.append(pltpu.make_async_remote_copy(
            src_ref=dc.at[levels, to], dst_ref=ret.at[me_z], send_sem=z_s.at[k - 1], recv_sem=z_r.at[k - 1],
            device_id=(me_d, to), device_id_type=MESH))
    for copy in returns:
        copy.start()
    ret[me_z] = dc[levels, me_z]

    for level in range(1, levels):
        for e in range(experts):
            advance(e, level)

    for copy in returns:
        copy.wait()
    dcomb = ret[...].reshape(nz * GROUP, tok)
    dsel = (dcomb - jnp.sum(comb * dcomb, axis=0, keepdims=True)) / wsum
    spread = jnp.where(chosen > 0.5, dsel, 0.0)
    gl_ref[...] = probs * (spread - jnp.sum(sel * spread, axis=0, keepdims=True))


def per_device(out_grad, logits, routes, hidden, w_down):
    tok, cols = out_grad.shape
    experts, slot_count, units = hidden.shape
    nz, nd = lax.axis_size("expert"), lax.axis_size("dp")
    cap, own = slot_count // nz, slot_count // nd
    pad = -(-own // 16) * 16
    rows, levels = nd * pad, nd.bit_length() - 1
    ft = next(f for f in (512, 384, 256, 128) if units % f == 0)

    lt = logits.T.reshape(nz, experts, tok)
    lt = jnp.pad(lt, ((0, 0), (0, GROUP - experts), (0, 0)), constant_values=-1e30).reshape(nz * GROUP, tok)
    hid = hidden.reshape(experts, nd, own, units)
    if pad != own:
        hid = jnp.pad(hid, ((0, 0), (0, 0), (0, pad - own), (0, 0)))
    vmem, hbm = pl.BlockSpec(memory_space=pltpu.VMEM), pl.BlockSpec(memory_space=pl.ANY)
    dma = lambda n: pltpu.SemaphoreType.DMA((n,))
    gh, gl, scaled = pl.pallas_call(
        functools.partial(kernel, nz, nd, own, pad, cap, experts, ft),
        out_shape=(
            jax.ShapeDtypeStruct((experts, pad, units), BF16),
            jax.ShapeDtypeStruct((nz * GROUP, tok), F32),
            jax.ShapeDtypeStruct((experts, nd, pad, cols), BF16),
        ),
        in_specs=[vmem, vmem, vmem, hbm, hbm],
        out_specs=(vmem, vmem, vmem),
        scratch_shapes=[
            pltpu.VMEM((experts, units, cols), BF16),
            pltpu.VMEM((experts, nd, pad, units), BF16),
            pltpu.VMEM((nz, tok, cols), BF16),
            pltpu.VMEM((nz, 2 * GROUP, tok), BF16),
            pltpu.VMEM((nz, 2 * GROUP, tok), BF16),
            pltpu.VMEM((experts, rows, nz * tok), BF16),
            pltpu.VMEM((rows, cols), BF16),
            pltpu.VMEM((experts, rows, tok), F32),
            pltpu.VMEM((experts, rows // 2, units), F32),
            pltpu.VMEM((experts, rows, units), BF16),
            pltpu.VMEM((experts, rows, units), BF16),
            pltpu.VMEM((rows, 128), F32),
            pltpu.VMEM((levels + 1, nz, GROUP, tok), F32),
            pltpu.VMEM((levels, nz, GROUP, tok), F32),
            pltpu.VMEM((nz, GROUP, tok), F32),
            dma(2 * experts), dma(nz - 1), dma(nz - 1), dma(nz - 1), dma(nz - 1),
            dma(experts * levels), dma(experts * levels), dma(levels), dma(levels), dma(nz - 1), dma(nz - 1),
        ],
        compiler_params=pltpu.CompilerParams(
            collective_id=0, has_side_effects=True, vmem_limit_bytes=60 * 1024 * 1024),
    )(out_grad, lt, routes.T, hid, w_down)

    grad_down = jnp.einsum(
        "ecsf,ecsd->efd", hid, scaled, preferred_element_type=F32) if pad != own else jnp.einsum(
        "esf,esd->efd", hidden, scaled.reshape(experts, slot_count, cols), preferred_element_type=F32)
    grad_hidden = jnp.transpose(gh[:, :own], (1, 0, 2))
    grad_logits = gl.reshape(nz, GROUP, tok)[:, :experts].reshape(nz * experts, tok).T
    return grad_down.astype(BF16), grad_hidden, grad_logits


def solution(mesh):
    return jax.shard_map(
        per_device,
        mesh=mesh,
        in_specs=(
            P("expert", "dp"),
            P("expert", None),
            P("expert", None),
            P("expert", None, None),
            P("expert", None, "dp"),
        ),
        out_specs=(P("expert", None, "dp"), P("dp", "expert", None), P("expert", None)),
        check_vma=False,
    )
```

time: 159 us -> 71.5 us (0.45)
  blocking collectives: 56.6 us -> 0 us
  Pallas kernels: 0 us -> 47.9 us
  local copies, waits for them, and re-layouts: 40.8 us -> 13.6 us
  between operations: 14.2 us -> 0.64 us
  matrix products: 22 us -> 8.93 us
  waiting for transfers between devices: 10.5 us -> 0 us
  other arithmetic: 7.55 us -> 0 us
  starting transfers between devices: 6.71 us -> 0 us
    pallas_call x0 -> x1, Pallas kernels: none -> 47.9 us  [per_device(): pl.pallas_call(functools.partial(kernel, nz, nd, own, pad, cap, experts,...]
    all_to_all x1 -> x0, blocking collectives: 43.3 us -> none  [per_device(): lax.all_to_all(send_rows, 'expert', split_axis=0, concat_axis=1, tiled=True)]
    gather x6 -> x0, local copies, waits for them, and re-layouts: 13.5 us -> none  [the longest x5 7.35 us: per_device(): sel = jnp.take_along_axis(probs, routes, axis=1)]
    psum x1 -> x0, blocking collectives: 13.3 us -> none  [per_device(): dslot = lax.psum(local_part, 'dp')]
    scatter x2 -> x0, local copies, waits for them, and re-layouts: 13.2 us -> none  [the longest x1 7.59 us: per_device(): jnp.zeros((n_experts * capacity,), jnp.bfloat16).at[target]]
    dot_general x3 -> x1, matrix products: 22 us -> 8.93 us  [per_device(): jnp.einsum('esf,esd->efd', hidden, scaled.reshape(experts, slot_count, co...]
    all_to_all x2 -> x0, waiting for transfers between devices: 10.5 us -> none  [the longest x1 5.54 us: per_device(): lax.all_to_all(dslot, 'expert', split_axis=1, concat_axis=0, tiled=True)]
    all_to_all x2 -> x0, starting transfers between devices: 6.68 us -> none  [the longest x1 3.43 us: per_device(): lax.all_to_all(send_wts, 'expert', split_axis=0, concat_axis=1, tiled=True)]
  transfers between devices with their start and end apart: 3 -> 0, of which waited for: 2 -> 0; matrix products, arithmetic and copies ran while one was open for 31% -> 0% of each run, Pallas kernels for 0% -> 0%
where the time goes in v1:
time: 71.5 us; the launch traced here: 71 us
  Pallas kernels  47.9 us (67%)
  local copies, waits for them, and re-layouts  13.6 us (19%)
  matrix products  8.93 us (12%)
    pallas_call x1, Pallas kernels, per_device(): pl.pallas_call(functools.partial(kernel, nz, nd, own, pad, cap, experts,...  47.9 us
    unnamed x2, local copies, waits for them, and re-layouts  11 us
    dot_general x1, matrix products, per_device(): jnp.einsum('esf,esd->efd', hidden, scaled.reshape(experts, slot_count, co...  8.93 us

profile of v1, /device:TPU:0, one launch (start us, length us, event | category | flops | bytes accessed | tf_op | source)
XLA Modules:
  0.0 71.0 jit_solution(15608109319018628662)
XLA Ops:
  0.6 1.3 %pad_bitcast_fusion.lt_ref = f32[32,128]{1,0:T(8,128)} fusion(f32[4,4,128]{2,1,0:T(4,128)} %bitcast.20), kind=kLoop, calls=%fused_computation.1 | loop fusion | bytes 24576 | tf_op jit(solution)/shard_map/reshape | solution.py:255
  1.9 47.9 %shard_map.76 = (bf16[4,48,1536]{2,1,0:T(8,128)(2,1)}, f32[32,128]{1,0:T(8,128)}, bf16[4,8,48,512]{3,2,1,0:T(8,128)(2,1)}) custom-call(bf16[128,512]{1,0:T(8,128)(2,1)} %og_ref.1, f32[32,128]{1,0:T(8,128)} %pad_bitcast_fusion.lt_ref, s32[8,128]{1,0:T(8,128)} %bitcast.22, bf16[4,8,48,1536]{3,2,1,0:T(8,128)(2,1)} %bitcast.17, bf16[4,1536,512]{2,1,0:T(8,128)(2,1)} %w_hbm.1), custom_call_target="tpu_custom_call" | custom-call | tf_op jit(solution)/shard_map/pallas_call | solution.py:261
  49.8 2.3 %copy.10 = bf16[48,4,1536]{2,1,0:T(4,128)(2,1)} copy(bf16[48,4,1536]{2,0,1:T(8,128)(2,1)} %bitcast.19) | data formatting | bytes 1179648
  52.1 1.3 %slice.4 = f32[4,4,128]{2,1,0:T(4,128)} slice(f32[4,8,128]{2,1,0:T(8,128)} %bitcast.23), slice={[0:4], [0:4], [0:128]} | slice | bytes 16384 | tf_op jit(solution)/shard_map/slice | solution.py:297
  53.5 8.9 %convert_bitcast_fusion = bf16[4,1536,512]{1,2,0:T(8,128)(2,1)} fusion(bf16[4,384,512]{2,1,0:T(8,128)(2,1)} %bitcast.18, bf16[4,384,1536]{2,1,0:T(8,128)(2,1)} %param.8), kind=kOutput, calls=%fused_computation | convolution fusion | flops 2419064832 | bytes 12582912 | tf_op jit(solution)/shard_map/esf,esd->efd/dot_general | solution.py:294
  62.4 8.6 %copy.9 = bf16[4,1536,512]{2,1,0:T(8,128)(2,1)} copy(bf16[4,1536,512]{1,2,0:T(8,128)(2,1)} %convert_bitcast_fusion) | data formatting | bytes 12582912

commit v2 on v1

--- a/solution.py
+++ b/solution.py
@@ -34,7 +34,7 @@
     nz, nd, own, pad, cap, experts, ft,
     og_ref, lt_ref, rt_ref, hid_hbm, w_hbm,
     gh_ref, gl_ref, scaled_ref,
-    w, hid, og, meta, gmeta, onehot, disp, wcol, acc, snd, rcv, dsl, dc, dcr, ret,
+    w, hid, og, meta, gmeta, onehot, disp, wcol, acc, snd, rcv, dsl, dc, dcr, ret, lt_pad,
     load_sem, og_s, og_r, mt_s, mt_r, rs_s, rs_r, ar_s, ar_r, z_s, z_r,
 ):
     me_d, me_z = lax.axis_index("dp"), lax.axis_index("expert")
@@ -60,7 +60,10 @@
     for b in range(levels):
         pl.semaphore_signal(barrier, inc=1, device_id=(flipped(me_d, b), me_z), device_id_type=MESH)
 
-    lt = lt_ref[...]
+    lt_pad[...] = jnp.full(lt_pad.shape, -1e30, F32)
+    for z in range(nz):
+        lt_pad[z * GROUP : z * GROUP + experts] = lt_ref[z * experts : (z + 1) * experts]
+    lt = lt_pad[...]
     row = lax.broadcasted_iota(jnp.int32, lt.shape, 0)
     local = lax.rem(row, GROUP)
     eid = jnp.where(local < experts, (row // GROUP) * experts + local, -1)
@@ -197,7 +200,7 @@
             acc[e, 0:keep] += rcv[e, start : start + keep].astype(F32)
         else:
             total = acc[e, 0:size] + rcv[e, start : start + size].astype(F32)
-            gh_ref[e] = (wcol[e, 0:size, 0:1] * total).astype(BF16)
+            gh_ref[:, e, :] = (wcol[e, 0:size, 0:1] * total).astype(BF16)[:own]
 
     def ar_copy(level):
         return pltpu.make_async_remote_copy(
@@ -239,7 +242,20 @@
     dcomb = ret[...].reshape(nz * GROUP, tok)
     dsel = (dcomb - jnp.sum(comb * dcomb, axis=0, keepdims=True)) / wsum
     spread = jnp.where(chosen > 0.5, dsel, 0.0)
-    gl_ref[...] = probs * (spread - jnp.sum(sel * spread, axis=0, keepdims=True))
+    out = probs * (spread - jnp.sum(sel * spread, axis=0, keepdims=True))
+    for z in range(nz):
+        gl_ref[z * experts : (z + 1) * experts] = out[z * GROUP : z * GROUP + experts]
+
+
+def grad_kernel(hid_ref, scaled_ref, gh_ref, gl_ref, gd_out, gh_out, gl_out):
+    @pl.when(pl.program_id(1) == 0)
+    def _():
+        gh_out[...] = gh_ref[...]
+        gl_out[...] = gl_ref[...]
+
+    h = hid_ref[0].reshape(-1, hid_ref.shape[-1])
+    x = scaled_ref[0].reshape(-1, scaled_ref.shape[-1])
+    gd_out[0] = lax.dot_general(h, x, (((0,), (0,)), ((), ())), preferred_element_type=F32).astype(BF16)
 
 
 def per_device(out_grad, logits, routes, hidden, w_down):
@@ -251,8 +267,6 @@
     rows, levels = nd * pad, nd.bit_length() - 1
     ft = next(f for f in (512, 384, 256, 128) if units % f == 0)
 
-    lt = logits.T.reshape(nz, experts, tok)
-    lt = jnp.pad(lt, ((0, 0), (0, GROUP - experts), (0, 0)), constant_values=-1e30).reshape(nz * GROUP, tok)
     hid = hidden.reshape(experts, nd, own, units)
     if pad != own:
         hid = jnp.pad(hid, ((0, 0), (0, 0), (0, pad - own), (0, 0)))
@@ -261,8 +275,8 @@
     gh, gl, scaled = pl.pallas_call(
         functools.partial(kernel, nz, nd, own, pad, cap, experts, ft),
         out_shape=(
-            jax.ShapeDtypeStruct((experts, pad, units), BF16),
-            jax.ShapeDtypeStruct((nz * GROUP, tok), F32),
+            jax.ShapeDtypeStruct((own, experts, units), BF16),
+            jax.ShapeDtypeStruct((nz * experts, tok), F32),
             jax.ShapeDtypeStruct((experts, nd, pad, cols), BF16),
         ),
         in_specs=[vmem, vmem, vmem, hbm, hbm],
@@ -283,19 +297,37 @@
             pltpu.VMEM((levels + 1, nz, GROUP, tok), F32),
             pltpu.VMEM((levels, nz, GROUP, tok), F32),
             pltpu.VMEM((nz, GROUP, tok), F32),
+            pltpu.VMEM((nz * GROUP, tok), F32),
             dma(2 * experts), dma(nz - 1), dma(nz - 1), dma(nz - 1), dma(nz - 1),
             dma(experts * levels), dma(experts * levels), dma(levels), dma(levels), dma(nz - 1), dma(nz - 1),
         ],
         compiler_params=pltpu.CompilerParams(
             collective_id=0, has_side_effects=True, vmem_limit_bytes=60 * 1024 * 1024),
-    )(out_grad, lt, routes.T, hid, w_down)
-
-    grad_down = jnp.einsum(
-        "ecsf,ecsd->efd", hid, scaled, preferred_element_type=F32) if pad != own else jnp.einsum(
-        "esf,esd->efd", hidden, scaled.reshape(experts, slot_count, cols), preferred_element_type=F32)
-    grad_hidden = jnp.transpose(gh[:, :own], (1, 0, 2))
-    grad_logits = gl.reshape(nz, GROUP, tok)[:, :experts].reshape(nz * experts, tok).T
-    return grad_down.astype(BF16), grad_hidden, grad_logits
+    )(out_grad, logits.T, routes.T, hid, w_down)
+
+    gt = next(f for f in (768, 512, 384, 256, 128) if units % f == 0)
+    grad_down, grad_hidden, grad_logits = pl.pallas_call(
+        grad_kernel,
+        grid=(experts, units // gt),
+        in_specs=[
+            pl.BlockSpec((1, nd, pad, gt), lambda e, i: (e, 0, 0, i)),
+            pl.BlockSpec((1, nd, pad, cols), lambda e, i: (e, 0, 0, 0)),
+            pl.BlockSpec((own // experts, experts, units), lambda e, i: (e, 0, 0)),
+            pl.BlockSpec(gl.shape, lambda e, i: (0, 0)),
+        ],
+        out_specs=(
+            pl.BlockSpec((1, gt, cols), lambda e, i: (e, i, 0)),
+            pl.BlockSpec((own // experts, experts, units), lambda e, i: (e, 0, 0)),
+            pl.BlockSpec(gl.shape, lambda e, i: (0, 0)),
+        ),
+        out_shape=(
+            jax.ShapeDtypeStruct((experts, units, cols), BF16),
+            jax.ShapeDtypeStruct((own, experts, units), BF16),
+            jax.ShapeDtypeStruct(gl.shape, F32),
+        ),
+        compiler_params=pltpu.CompilerParams(vmem_limit_bytes=60 * 1024 * 1024),
+    )(hid, scaled, gh, gl)
+    return grad_down, grad_hidden, grad_logits.T
 
 
 def solution(mesh):

time: 71.5 us -> 59 us (0.83)
  local copies, waits for them, and re-layouts: 13.6 us -> 0 us
  Pallas kernels: 47.9 us -> 58.1 us
  matrix products: 8.93 us -> 0 us
    unnamed x2 -> x0, local copies, waits for them, and re-layouts: 11 us -> none
    pallas_call x0 -> x1, Pallas kernels: none -> 10 us  [per_device(): pl.pallas_call(grad_kernel, grid=(experts, units // gt), in_specs=[pl.Blo...]
    dot_general x1 -> x0, matrix products: 8.93 us -> none  [per_device(): jnp.einsum('esf,esd->efd', hidden, scaled.reshape(experts, slot_count, co...]
    slice x1 -> x0, local copies, waits for them, and re-layouts: 1.32 us -> none  [per_device(): gl.reshape(nz, GROUP, tok)[:, :experts].reshape(nz * experts, tok)]
    reshape x1 -> x0, local copies, waits for them, and re-layouts: 1.31 us -> none  [per_device(): jnp.pad(lt, ((0, 0), (0, GROUP - experts), (0, 0)), constant_values=-1e+30)]
where the time goes in v2:
time: 59 us; the launch traced here: 58.7 us
  Pallas kernels  58.1 us (98%)
  between operations  0.64 us (1%)
    pallas_call x1, Pallas kernels, per_device(): pl.pallas_call(functools.partial(kernel, nz, nd, own, pad, cap, experts,...  48 us
    pallas_call x1, Pallas kernels, per_device(): pl.pallas_call(grad_kernel, grid=(experts, units // gt), in_specs=[pl.Blo...  10 us

profile of v2, /device:TPU:0, one launch (start us, length us, event | category | flops | bytes accessed | tf_op | source)
XLA Modules:
  0.0 58.7 jit_solution(17428614681115321080)
XLA Ops:
  0.6 48.0 %shard_map.76 = (bf16[48,4,1536]{2,1,0:T(4,128)(2,1)}, f32[16,128]{1,0:T(8,128)}, bf16[4,8,48,512]{3,2,1,0:T(8,128)(2,1)}) custom-call(bf16[128,512]{1,0:T(8,128)(2,1)} %og_ref.1, f32[16,128]{1,0:T(8,128)} %bitcast.6, s32[8,128]{1,0:T(8,128)} %bitcast.7, bf16[4,8,48,1536]{3,2,1,0:T(8,128)(2,1)} %bitcast.4, bf16[4,1536,512]{2,1,0:T(8,128)(2,1)} %w_hbm.1), custom_call_target="tpu_custom_call" | custom-call | tf_op jit(solution)/shard_map/pallas_call | solution.py:275
  48.6 10.0 %shard_map.77 = (bf16[4,1536,512]{2,1,0:T(8,128)(2,1)}, bf16[48,4,1536]{2,1,0:T(4,128)(2,1)}, f32[16,128]{1,0:T(8,128)}) custom-call(bf16[4,8,48,1536]{3,2,1,0:T(8,128)(2,1)} %bitcast.5, bf16[4,8,48,512]{3,2,1,0:T(8,128)(2,1)} %get-tuple-element.9.scaled_ref, bf16[48,4,1536]{2,1,0:T(4,128)(2,1)} %get-tuple-element.10.gh_ref, f32[16,128]{1,0:T(8,128)} %get-tuple-element.11.gl_ref), custom_call_target="tpu_custom_call" | custom-call | tf_op jit(solution)/shard_map/pallas_call | solution.py:309

commit v3 on v2

--- a/solution.py
+++ b/solution.py
@@ -271,6 +271,7 @@
     if pad != own:
         hid = jnp.pad(hid, ((0, 0), (0, 0), (0, pad - own), (0, 0)))
     vmem, hbm = pl.BlockSpec(memory_space=pltpu.VMEM), pl.BlockSpec(memory_space=pl.ANY)
+    far = pl.BlockSpec(memory_space=pltpu.HBM)
     dma = lambda n: pltpu.SemaphoreType.DMA((n,))
     gh, gl, scaled = pl.pallas_call(
         functools.partial(kernel, nz, nd, own, pad, cap, experts, ft),
@@ -279,7 +280,7 @@
             jax.ShapeDtypeStruct((nz * experts, tok), F32),
             jax.ShapeDtypeStruct((experts, nd, pad, cols), BF16),
         ),
-        in_specs=[vmem, vmem, vmem, hbm, hbm],
+        in_specs=[vmem, vmem, vmem, far, far],
         out_specs=(vmem, vmem, vmem),
         scratch_shapes=[
             pltpu.VMEM((experts, units, cols), BF16),
@@ -302,7 +303,7 @@
             dma(experts * levels), dma(experts * levels), dma(levels), dma(levels), dma(nz - 1), dma(nz - 1),
         ],
         compiler_params=pltpu.CompilerParams(
-            collective_id=0, has_side_effects=True, vmem_limit_bytes=60 * 1024 * 1024),
+            collective_id=0, has_side_effects=True, vmem_limit_bytes=(44 if nz * tok <= 1024 else 60) * 1024 * 1024),
     )(out_grad, logits.T, routes.T, hid, w_down)
 
     gt = next(f for f in (768, 512, 384, 256, 128) if units % f == 0)
@@ -325,7 +326,7 @@
             jax.ShapeDtypeStruct((own, experts, units), BF16),
             jax.ShapeDtypeStruct(gl.shape, F32),
         ),
-        compiler_params=pltpu.CompilerParams(vmem_limit_bytes=60 * 1024 * 1024),
+        compiler_params=pltpu.CompilerParams(vmem_limit_bytes=16 * 1024 * 1024),
     )(hid, scaled, gh, gl)
     return grad_down, grad_hidden, grad_logits.T
 

time: 59 us -> 59.1 us (level)
  local copies, waits for them, and re-layouts: 0 us -> 4.62 us
  Pallas kernels: 58.1 us -> 53.6 us
    unnamed x0 -> x8, local copies, waits for them, and re-layouts: none -> 4.62 us
    pallas_call x1, Pallas kernels: 10 us -> 6.88 us  [per_device(): pl.pallas_call(grad_kernel, grid=(experts, units // gt), in_specs=[pl.Blo...]
    pallas_call x1, Pallas kernels: 48 us -> 46.7 us  [per_device(): pl.pallas_call(functools.partial(kernel, nz, nd, own, pad, cap, experts,...]
where the time goes in v3:
time: 59.1 us; the launch traced here: 58.9 us
  Pallas kernels  53.6 us (91%)
  local copies, waits for them, and re-layouts  4.62 us (8%)
  between operations  0.65 us (1%)
    pallas_call x1, Pallas kernels, per_device(): pl.pallas_call(functools.partial(kernel, nz, nd, own, pad, cap, experts,...  46.7 us
    pallas_call x1, Pallas kernels, per_device(): pl.pallas_call(grad_kernel, grid=(experts, units // gt), in_specs=[pl.Blo...  6.88 us
    unnamed x8, local copies, waits for them, and re-layouts  4.62 us

profile of v3, /device:TPU:0, one launch (start us, length us, event | category | flops | bytes accessed | tf_op | source)
XLA Modules:
  0.0 58.9 jit_solution(7317294999200823017)
XLA Ops:
  0.6 0.0 copy-start
  0.6 2.3 %copy-done = bf16[4,384,1536]{2,1,0:T(8,128)(2,1)S(1)} copy-done((bf16[4,384,1536]{2,1,0:T(8,128)(2,1)S(1)}, bf16[4,384,1536]{2,1,0:T(8,128)(2,1)}, u32[]{:S(2)}) %copy-start) | copy-done | bytes 4718616
  3.0 0.0 copy-start.1
  3.0 0.9 %copy-done.1 = bf16[128,512]{1,0:T(8,128)(2,1)S(1)} copy-done((bf16[128,512]{1,0:T(8,128)(2,1)S(1)}, bf16[128,512]{1,0:T(8,128)(2,1)}, u32[]{:S(2)}) %copy-start.1) | copy-done | bytes 131096
  3.9 0.0 copy-start.2
  3.9 0.7 %copy-done.2 = f32[128,16]{0,1:T(8,128)S(1)} copy-done((f32[128,16]{0,1:T(8,128)S(1)}, f32[128,16]{0,1:T(8,128)}, u32[]{:S(2)}) %copy-start.2) | copy-done | bytes 8216
  4.6 0.0 copy-start.3
  4.6 0.7 %copy-done.3 = s32[128,8]{0,1:T(8,128)S(1)} copy-done((s32[128,8]{0,1:T(8,128)S(1)}, s32[128,8]{0,1:T(8,128)}, u32[]{:S(2)}) %copy-start.3) | copy-done | bytes 4120
  5.3 46.7 %shard_map.76 = (bf16[48,4,1536]{2,1,0:T(4,128)(2,1)S(1)}, f32[16,128]{1,0:T(8,128)S(1)}, bf16[4,8,48,512]{3,2,1,0:T(8,128)(2,1)S(1)}) custom-call(bf16[128,512]{1,0:T(8,128)(2,1)S(1)} %copy-done.1, f32[16,128]{1,0:T(8,128)S(1)} %bitcast.6, s32[8,128]{1,0:T(8,128)S(1)} %bitcast.7, bf16[4,8,48,1536]{3,2,1,0:T(8,128)(2,1)S(1)} %bitcast.4, ...), custom_call_target="tpu_custom_call" | custom-call | tf_op jit(solution)/shard_map/pallas_call | solution.py:276
  52.0 6.9 %shard_map.77 = (bf16[4,1536,512]{2,1,0:T(8,128)(2,1)}, bf16[48,4,1536]{2,1,0:T(4,128)(2,1)}, f32[16,128]{1,0:T(8,128)}) custom-call(bf16[4,8,48,1536]{3,2,1,0:T(8,128)(2,1)S(1)} %bitcast.5, bf16[4,8,48,512]{3,2,1,0:T(8,128)(2,1)S(1)} %get-tuple-element.9.scaled_ref, bf16[48,4,1536]{2,1,0:T(4,128)(2,1)S(1)} %get-tuple-element.10.gh_ref, ...), custom_call_target="tpu_custom_call" | custom-call | tf_op jit(solution)/shard_map/pallas_call | solution.py:310
Async XLA Ops:
  0.6 2.3 %copy-start = (bf16[4,384,1536]{2,1,0:T(8,128)(2,1)S(1)}, bf16[4,384,1536]{2,1,0:T(8,128)(2,1)}, u32[]{:S(2)}) copy-start(bf16[4,384,1536]{2,1,0:T(8,128)(2,1)} %param.8) | copy-start | bytes 14155780
  3.0 0.9 %copy-start.1 = (bf16[128,512]{1,0:T(8,128)(2,1)S(1)}, bf16[128,512]{1,0:T(8,128)(2,1)}, u32[]{:S(2)}) copy-start(bf16[128,512]{1,0:T(8,128)(2,1)} %og_ref.1) | copy-start | bytes 393220
  3.9 0.7 %copy-start.2 = (f32[128,16]{0,1:T(8,128)S(1)}, f32[128,16]{0,1:T(8,128)}, u32[]{:S(2)}) copy-start(f32[128,16]{0,1:T(8,128)} %param.6) | copy-start | bytes 24580
  4.6 0.7 %copy-start.3 = (s32[128,8]{0,1:T(8,128)S(1)}, s32[128,8]{0,1:T(8,128)}, u32[]{:S(2)}) copy-start(s32[128,8]{0,1:T(8,128)} %param.7) | copy-start | bytes 12292
